TPU v7x, 128 devices: a whole 4x4x4 slice. The times are simulated.
128 devices in a mesh: tm: 32 (over y, z, core), feat: 4 (over x).
Axes of the slice: x: 4, y: 4, z: 4, core: 2. Of those that a mesh axis runs over, the one named last changes fastest.
Arguments:
- snapshots: bfloat16 [8192, 512], P('tm'), may hold values from -6 to 6
- projection: bfloat16 [4096, 8192], P(None, 'feat'), may hold values from -0.09375 to 0.09375
- phase_shift: float32 [8192], P('feat'), may hold values from -3.140625 to 3.140625
Outputs:
- gram: float32 [8192, 2048], P('feat', 'tm')
- cross: float32 [8192, 2048], P('feat', 'tm')
All inputs are finite; a program needn't handle non-finite values.
Results may differ from a plain program's by a relative error of at most 0.0003.
Values may be sent and summed in bfloat16 or wider, within the bound.
No kernel may reach another device: no remote copies, remote signals or barrier semaphores. Data moves between devices by JAX's collectives and lax.ppermute only.
A program may use at most 128 MiB of HBM per device.

v0:
```python
import math

import jax
import jax.numpy as jnp
from jax import lax
from jax.sharding import PartitionSpec as P

CWD = 512


root_two = math.sqrt(2.0)


def from_behind(value, axis, by):
    devices = lax.axis_size(axis)
    pairs = [(i, i + by) for i in range(devices) if 0 <= i + by < devices]
    return lax.ppermute(value, axis, pairs)


def contract(left, right):
    return lax.dot_general(
        left,
        right,
        (((0,), (0,)), ((), ())),
        precision=lax.Precision.HIGHEST,
        preferred_element_type=jnp.float32,
    )


def local(snapshots, projection, phase_shift):
    num_rows = snapshots.shape[0]
    pc_count = snapshots.shape[1]
    lag_count = projection.shape[0] // pc_count
    tm_count = lax.axis_size("tm")
    position = lax.axis_index("tm")
    history = from_behind(snapshots[num_rows - (lag_count - 1) :], "tm", 1)
    extended = jnp.concatenate([history, snapshots], 0)
    embedded = jnp.concatenate(
        [extended[lag_count - 1 - k : lag_count - 1 - k + num_rows] for k in range(lag_count)], 1
    )
    projected = jnp.dot(embedded, projection, preferred_element_type=jnp.float32) + phase_shift
    feats = root_two * jnp.cos(projected)
    gathered = lax.all_gather(feats[:, :CWD], "feat", axis=1, tiled=True)
    edge_row = from_behind(gathered[:1], "tm", -1)
    later = jnp.concatenate([gathered[1:], edge_row], 0)
    keep_mask = jnp.logical_or(jnp.arange(num_rows) < num_rows - 1, position < tm_count - 1)
    later = later * keep_mask.astype(later.dtype)[:, None]
    total_steps = num_rows * tm_count
    gram_term = contract(feats, gathered)
    cross_term = contract(feats, later)
    gram_part, cross_part = (
        lax.psum_scatter(gram_term, "tm", scatter_dimension=1, tiled=True),
        lax.psum_scatter(cross_term, "tm", scatter_dimension=1, tiled=True),
    )
    return (gram_part / total_steps, cross_part / (total_steps - 1))


def solution(mesh):
    in_specs = (P("tm", None), P(None, "feat"), P("feat"))
    out_specs = (P("feat", "tm"), P("feat", "tm"))
    return jax.shard_map(local, mesh=mesh, in_specs=in_specs, out_specs=out_specs, check_vma=False)
```

profile of v0, /device:TPU:1, one launch (start us, length us, event | category | flops | bytes accessed | tf_op | source)
XLA Modules:
  0.0 323.8 jit_solution(10617155344449154389)
XLA Ops:
  7.2 0.0 copy-start
  7.2 0.0 all-gather.2.cloned.1.call-start
  7.2 0.7 slice.33
  8.0 0.0 copy-start.1
  8.0 5.1 %collective-permute-start = (bf16[7,512]{1,0:T(8,128)(2,1)S(1)}, bf16[7,512]{1,0:T(8,128)(2,1)S(1)}, u32[]{:S(2)}, u32[]{:S(2)}) collective-permute-start(bf16[7,512]{1,0:T(8,128)(2,1)S(1)} %slice.33), channel_id=1, source_target_pairs={{0,4},{4,8},{8,12},{12,16},{16,20},{20,24},{24,28},{28,32},{32,36}... | collective-permute-start | bytes 21512 | tf_op jit(solution)/shard_map/ppermute | solution.py:17
  13.0 1.0 constant_dynamic-update-slice_fusion
  14.0 0.0 collective-permute-done
  14.0 1.0 fusion.9
  15.0 1.0 fusion.11
  16.1 1.0 fusion.13
  17.1 0.0 copy-done
  17.1 0.1 fusion.15
  17.2 0.1 fusion.17
  17.2 0.1 fusion.7
  17.3 0.1 fusion.18
  17.4 0.0 copy-done.1
  17.4 13.7 %fusion.1 = f32[256,2048]{1,0:T(8,128)S(1)} fusion(bf16[256,4096]{1,0:T(8,128)(2,1)S(1)} %fusion.18, bf16[4096,2048]{1,0:T(8,128)(2,1)} %param.4, f32[2048]{0:T(1024)S(1)} %copy-done.1), kind=kOutput, calls=%fused_computation.2 | convolution fusion | flops 4296015872 | bytes 20979712 | tf_op jit(solution)/shard_map/dot_general | solution.py:41
  31.1 0.8 slice.56
  32.0 0.0 all-gather.2.cloned.1.call-update
  32.0 0.0 reduce-scatter.3.cloned.1.call-start
  32.0 33.2 %all-gather.2.cloned.1.call-done = f32[256,2048]{1,0:T(8,128)} async-done(((f32[256,512]{1,0:T(8,128)}), f32[256,2048]{1,0:T(8,128)}) %all-gather.2.cloned.1.call-update) | async-done | bytes 2097168 | tf_op jit(solution)/shard_map/all_gather | solution.py:43
  65.2 17.3 %fusion.20 = f32[2048,2048]{0,1:T(8,128)} fusion(f32[256,2048]{1,0:T(8,128)S(1)} %fusion.1, f32[256,2048]{1,0:T(8,128)} %all-gather.2.cloned.1.call-done), kind=kOutput, calls=%fused_computation.33 | convolution fusion | flops 12884901888 | bytes 20971520 | tf_op jit(solution)/shard_map/dot_general | solution.py:21
  82.5 0.0 reduce-scatter.3.cloned.1.call-update
  82.6 0.0 reduce-scatter.5.cloned.1.call-start
  82.6 0.8 slice.58
  83.5 2.6 collective-permute-start.1
  86.1 1.9 slice.57
  87.9 0.6 collective-permute-done.1
  88.5 16.3 %fusion.2 = f32[2048,2048]{0,1:T(8,128)} fusion(f32[256,2048]{1,0:T(8,128)S(1)} %fusion.1, f32[1,2048]{1,0:T(1,128)S(1)} %collective-permute-done.1, f32[255,2048]{1,0:T(8,128)S(1)} %slice.57, f32[256]{0:T(256)S(1)} %or_convert_fusion), kind=kOutput, calls=%fused_computation.4 | convolution fusion | flops 12885950464 | bytes 20972544 | tf_op jit(solution)/shard_map/dot_general | solution.py:21
  104.8 0.0 reduce-scatter.5.cloned.1.call-update
  104.8 92.0 %reduce-scatter.3.cloned.1.call-done = f32[2048,64]{0,1:T(8,128)} async-done(((f32[2048,2048]{0,1:T(8,128)}), f32[2048,64]{0,1:T(8,128)}) %reduce-scatter.3.cloned.1.call-update) | async-done | bytes 524304 | tf_op jit(solution)/shard_map/reduce_scatter | solution.py:52
  196.8 1.9 broadcast_multiply_fusion.1
  198.7 116.7 %reduce-scatter.5.cloned.1.call-done = f32[2048,64]{0,1:T(8,128)} async-done(((f32[2048,2048]{0,1:T(8,128)}), f32[2048,64]{0,1:T(8,128)}) %reduce-scatter.5.cloned.1.call-update) | async-done | bytes 524304 | tf_op jit(solution)/shard_map/reduce_scatter | solution.py:53
  315.4 1.9 broadcast_multiply_fusion
  (1 shorter events, 0.0 us)
Async XLA Ops:
  7.2 9.9 %copy-start = (bf16[256,512]{1,0:T(8,128)(2,1)S(1)}, bf16[256,512]{1,0:T(8,128)(2,1)}, u32[]{:S(2)}) copy-start(bf16[256,512]{1,0:T(8,128)(2,1)} %param.3) | copy-start | bytes 786436
  7.2 58.0 %all-gather.2.cloned.1.call-start = ((), (), s32[]{:S(2)}) async-start(), calls=%async_computation.2 | async-start | bytes 2621440 | tf_op jit(solution)/shard_map/all_gather | solution.py:43
  8.0 9.4 %copy-start.1 = (f32[2048]{0:T(1024)S(1)}, f32[2048]{0:T(1024)}, u32[]{:S(2)}) copy-start(f32[2048]{0:T(1024)} %param.5) | copy-start | bytes 24580
  8.0 6.0 %collective-permute-start = (bf16[7,512]{1,0:T(8,128)(2,1)S(1)}, bf16[7,512]{1,0:T(8,128)(2,1)S(1)}, u32[]{:S(2)}, u32[]{:S(2)}) collective-permute-start(bf16[7,512]{1,0:T(8,128)(2,1)S(1)} %slice.33), channel_id=1, source_target_pairs={{0,4},{4,8},{8,12},{12,16},{16,20},{20,24},{24,28},{28,32},{32,36}... | collective-permute-start | bytes 21512 | tf_op jit(solution)/shard_map/ppermute | solution.py:17
  32.0 164.8 %reduce-scatter.3.cloned.1.call-start = ((), (), s32[]{:S(2)}) async-start(), calls=%async_computation.3 | async-start | bytes 17301504 | tf_op jit(solution)/shard_map/reduce_scatter | solution.py:52
  82.6 232.8 %reduce-scatter.5.cloned.1.call-start = ((), (), s32[]{:S(2)}) async-start(), calls=%async_computation.4 | async-start | bytes 17301504 | tf_op jit(solution)/shard_map/reduce_scatter | solution.py:53
  83.5 5.1 %collective-permute-start.1 = (f32[1,2048]{1,0:T(1,128)S(1)}, f32[1,2048]{1,0:T(1,128)S(1)}, u32[]{:S(2)}, u32[]{:S(2)}) collective-permute-start(f32[1,2048]{1,0:T(1,128)S(1)} %slice.58), channel_id=1, source_target_pairs={{4,0},{8,4},{12,8},{16,12},{20,16},{24,20},{28,24},{32,28},{36,32}... | collective-permute-start | bytes 24584 | tf_op jit(solution)/shard_map/ppermute | solution.py:17
Sparse Core Ops, SparseCore 0:
  32.1 33.0 all-gather.1
  82.7 114.0 reduce-scatter.2
  200.7 114.5 reduce-scatter.4
where the time goes:
time: 325 us; the launch traced here: 324 us
  waiting for transfers between devices  242 us (74%)
  matrix products  47.4 us (15%)
  between operations  13.9 us (4%)
  starting transfers between devices  7.75 us (2%)
  other arithmetic  7.08 us (2%)
  local copies, waits for them, and re-layouts  5.29 us (2%)
    reduce_scatter x1, waiting for transfers between devices, local(): lax.psum_scatter(cross_term, 'tm', scatter_dimension=1, tiled=True)  117 us
    reduce_scatter x1, waiting for transfers between devices, local(): lax.psum_scatter(gram_term, 'tm', scatter_dimension=1, tiled=True)  92 us
    dot_general x2, matrix products, contract(): lax.dot_general(left, right, (((0,), (0,)), ((), ())), precision=lax.Prec...  33.6 us
    all_gather x1, waiting for transfers between devices, local(): gathered = lax.all_gather(feats[:, :CWD], 'feat', axis=1, tiled=True)  33.2 us
    dot_general x1, matrix products, local(): jnp.dot(embedded, projection, preferred_element_type=jnp.float32)  13.7 us
    ppermute x2, starting transfers between devices, from_behind(): return lax.ppermute(value, axis, pairs)  7.63 us
  transfers between devices with their start and end apart: 5, of which 4 were waited for; matrix products, arithmetic and copies ran while one was open for 7% of the time, Pallas kernels for 0%

commit v1 on v0

v1 whole, which is shorter than its diff:
```python
import math

import jax
import jax.numpy as jnp
import numpy as np
from jax import lax
from jax.sharding import PartitionSpec as P

CWD = 512
Y, Z, C = 4, 4, 2
HALO = 8

TWO_PI_HIGH = 6.28125
TWO_PI_LOW = 2 * math.pi - TWO_PI_HIGH


def half_cos_terms():
    fit = np.polynomial.chebyshev.Chebyshev.interpolate(
        lambda q: np.cos(np.sqrt(q) / 2), 4, domain=[0.0, (math.pi * 1.0005) ** 2]
    )
    return [float(v * math.sqrt(2 * math.sqrt(2.0))) for v in fit.convert(kind=np.polynomial.Polynomial).coef]


TERMS = half_cos_terms()


def feature(angle):
    turns = jnp.round(angle * (1 / (2 * math.pi)))
    rest = (angle - turns * TWO_PI_HIGH) - turns * TWO_PI_LOW
    q = rest * rest
    p = TERMS[4]
    for term in TERMS[3::-1]:
        p = p * q + term
    return p * p - math.sqrt(2.0)


def move(value, to):
    pairs = []
    for y in range(Y):
        for z in range(Z):
            for c in range(C):
                goal = to(y, z, c)
                if goal is not None:
                    gy, gz, gc = goal
                    pairs.append(((y * Z + z) * C + c, (gy % Y * Z + gz % Z) * C + gc % C))
    return lax.ppermute(value, "tm", pairs)


def swap(value):
    return move(value, lambda y, z, c: (y, z, 1 - c))


def split(value):
    high = value.astype(jnp.bfloat16)
    return high, (value - high.astype(jnp.float32)).astype(jnp.bfloat16)


def contract(left, right):
    return lax.dot_general(left, right, (((0,), (0,)), ((), ())), preferred_element_type=jnp.float32)


def local(snapshots, projection, phase_shift):
    rows, pcs = snapshots.shape
    lags = projection.shape[0] // pcs
    position = lax.axis_index("tm")
    y, z, c = position // (Z * C), position // C % Z, position % C
    x = lax.axis_index("feat")

    width = CWD // Z
    mine = lax.dynamic_slice_in_dim(projection, z * width, width, 1)
    pairs = lambda by: [(i, (i + by) % 4) for i in range(4)]
    parts = [mine] + [lax.ppermute(mine, "feat", pairs(by)) for by in (1, 2, 3)]
    parts = jnp.stack(parts[::-1] + parts[::-1])
    parts = lax.dynamic_slice_in_dim(parts, 3 - x, 4, 0)
    window_projection = jnp.moveaxis(parts, 0, 1).reshape(projection.shape[0], CWD)
    shift_all = lax.all_gather(lax.dynamic_slice_in_dim(phase_shift, z * width, width, 0), "feat", axis=0, tiled=True)

    others = [move(snapshots, lambda y, z, c, by=by: (y, z + by, c)) for by in (1, 2, 3)]
    own = jnp.stack([snapshots] + others)
    other = swap(own)
    pair = jnp.where(c == 0, jnp.stack([own, other], 1), jnp.stack([other, own], 1))
    pair = pair.reshape(4, C * rows, pcs)[::-1]
    slab = lax.dynamic_slice_in_dim(jnp.concatenate([pair, pair]), 3 - z, 4, 0).reshape(-1, pcs)
    count = slab.shape[0]
    before = move(slab[-HALO:], lambda y, z, c: (y + 1, z, c) if y < Y - 1 else None)
    after = move(slab[:HALO], lambda y, z, c: (y - 1, z, c) if y > 0 else None)
    extended = jnp.concatenate([before, slab, after], 0)
    embedded = jnp.concatenate([extended[HALO - k : HALO - k + count + HALO] for k in range(lags)], 1)

    half = projection.shape[1] // C
    own_projection = lax.dynamic_slice_in_dim(projection, c * half, half, 1)
    own_shift = lax.dynamic_slice_in_dim(phase_shift, c * half, half, 0)
    feats = feature(jnp.dot(embedded[:count], own_projection, preferred_element_type=jnp.float32) + own_shift)
    window = feature(jnp.dot(embedded, window_projection, preferred_element_type=jnp.float32) + shift_all)
    later = window[1 : count + 1]
    later = jnp.where((jnp.arange(count) == count - 1)[:, None] & (y == Y - 1), 0.0, later)
    fh, fl = split(feats)

    def product(w):
        wh, wl = split(w)
        return contract(wh, fh) + contract(wl, fh) + contract(wh, fl)

    both = jnp.stack([product(window[:count]), product(later)]).reshape(2, Y, width, half)

    def piece(by):
        return lax.dynamic_index_in_dim(both, (y + by) % Y, 1, keepdims=False)

    far = piece(2)
    up = move(far[0], lambda y, z, c: (y + 1, z, c))
    down = move(far[1], lambda y, z, c: (y - 1, z, c))
    from_below = move(piece(1).at[0].add(up), lambda y, z, c: (y + 1, z, c))
    from_above = move(piece(3).at[1].add(down), lambda y, z, c: (y - 1, z, c))
    total = piece(0) + from_below + from_above

    part = width // C
    theirs = swap(lax.dynamic_slice_in_dim(total, (1 - c) * part, part, 1))
    ours = lax.dynamic_slice_in_dim(total, c * part, part, 1)
    whole = jnp.where(c == 0, jnp.concatenate([ours, theirs], 2), jnp.concatenate([theirs, ours], 2))
    steps = count * Y
    return whole[0].T / steps, whole[1].T / (steps - 1)


def solution(mesh):
    in_specs = (P("tm", None), P(None, "feat"), P("feat"))
    out_specs = (P("feat", "tm"), P("feat", "tm"))
    return jax.shard_map(local, mesh=mesh, in_specs=in_specs, out_specs=out_specs, check_vma=False)
```

time: 325 us -> 215 us (0.66)
  waiting for transfers between devices: 242 us -> 48.5 us
  blocking collectives: 0 us -> 43.6 us
  starting transfers between devices: 7.75 us -> 28.4 us
  local copies, waits for them, and re-layouts: 5.29 us -> 23.9 us
  between operations: 13.9 us -> 0.95 us
  matrix products: 47.4 us -> 56.3 us
  other arithmetic: 7.08 us -> 12.6 us
    reduce_scatter x2 -> x0, waiting for transfers between devices: 209 us -> none  [the longest x1 117 us: local(): lax.psum_scatter(cross_term, 'tm', scatter_dimension=1, tiled=True)]
    ppermute x2 -> x14, waiting for transfers between devices: 0.58 us -> 48.5 us  [the longest x11 29.2 us: move(): return lax.ppermute(value, 'tm', pairs)]
    all_gather x0 -> x1, blocking collectives: none -> 43.6 us  [local(): lax.all_gather(lax.dynamic_slice_in_dim(phase_shift, z * width, width, 0)...]
    all_gather x1 -> x0, waiting for transfers between devices: 33.2 us -> none  [local(): gathered = lax.all_gather(feats[:, :CWD], 'feat', axis=1, tiled=True)]
    ppermute x2 -> x14, starting transfers between devices: 7.63 us -> 28.4 us  [the longest x11 24.4 us: move(): return lax.ppermute(value, 'tm', pairs)]
    unnamed x5 -> x23, local copies, waits for them, and re-layouts: 0.98 us -> 15.5 us
    dot_general x3 -> x8, matrix products: 47.4 us -> 56.3 us  [the longest x1 27.1 us: local(): jnp.dot(embedded[:count], own_projection, preferred_element_type=jnp.floa...]
    slice x4 -> x1, local copies, waits for them, and re-layouts: 4.31 us -> 0.01 us  [local(): slab[-HALO:]]
  transfers between devices with their start and end apart: 5 -> 14, of which waited for: 4 -> 5; matrix products, arithmetic and copies ran while one was open for 7% -> 3% of each run, Pallas kernels for 0% -> 0%
where the time goes in v1:
time: 215 us; the launch traced here: 214 us
  matrix products  56.3 us (26%)
  waiting for transfers between devices  48.5 us (23%)
  blocking collectives  43.6 us (20%)
  starting transfers between devices  28.4 us (13%)
  local copies, waits for them, and re-layouts  23.9 us (11%)
  other arithmetic  12.6 us (6%)
    all_gather x1, blocking collectives, local(): lax.all_gather(lax.dynamic_slice_in_dim(phase_shift, z * width, width, 0)...  43.6 us
    ppermute x11, waiting for transfers between devices, move(): return lax.ppermute(value, 'tm', pairs)  29.2 us
    dot_general x1, matrix products, local(): jnp.dot(embedded[:count], own_projection, preferred_element_type=jnp.floa...  27.1 us
    ppermute x11, starting transfers between devices, move(): return lax.ppermute(value, 'tm', pairs)  24.4 us
    ppermute x3, waiting for transfers between devices, local(): parts = [mine] + [lax.ppermute(mine, 'feat', pairs(by)) for by in (1, 2, 3)]  19.3 us
    unnamed x23, local copies, waits for them, and re-layouts  15.5 us
    dot_general x6, matrix products, contract(): lax.dot_general(left, right, (((0,), (0,)), ((), ())), preferred_element_...  14.9 us
    dot_general x1, matrix products, local(): jnp.dot(embedded, window_projection, preferred_element_type=jnp.float32)  14.3 us
  transfers between devices with their start and end apart: 14, of which 5 were waited for; matrix products, arithmetic and copies ran while one was open for 3% of the time, Pallas kernels for 0%

profile of v1, /device:TPU:1, one launch (start us, length us, event | category | flops | bytes accessed | tf_op | source)
XLA Modules:
  0.0 214.2 jit_solution(3374871655476998966)
XLA Ops:
  0.7 1.3 constant_dynamic-slice_fusion.3
  2.0 0.5 copy.7
  2.6 3.4 %collective-permute-start.6 = (bf16[4096,128]{0,1:T(8,128)(2,1)S(1)}, bf16[4096,128]{0,1:T(8,128)(2,1)S(1)}, u32[]{:S(2)}, u32[]{:S(2)}) collective-permute-start(bf16[4096,128]{0,1:T(8,128)(2,1)S(1)} %copy.7), channel_id=1, source_target_pairs={{0,3},{1,0},{2,1},{3,2},{4,7},{5,4},{6,5},{7,6},{8,11},{9,8},{10,9... | collective-permute-start | bytes 3145736 | tf_op jit(solution)/shard_map/ppermute | solution.py:72
  5.9 3.8 %collective-permute-start.2 = (bf16[256,512]{1,0:T(8,128)(2,1)S(1)}, bf16[256,512]{1,0:T(8,128)(2,1)}, u32[]{:S(2)}, u32[]{:S(2)}) collective-permute-start(bf16[256,512]{1,0:T(8,128)(2,1)S(1)} %copy-done.2), channel_id=1, source_target_pairs={{0,24},{4,28},{8,0},{12,4},{16,8},{20,12},{24,16},{28,20},{32,56},... | collective-permute-start | bytes 786440 | tf_op jit(solution)/shard_map/ppermute | solution.py:46
  9.7 0.7 collective-permute-start
  10.4 0.5 collective-permute-start.7
  11.0 43.6 %all-gather = f32[4,1,128]{2,1,0:T(1,128)S(1)} all-gather(f32[1,1,128]{2,1,0:T(1,128)S(1)} %dynamic-slice_bitcast_fusion), channel_id=1, replica_groups=mesh['tm'=32,'feat'=4] {'feat'}, dimensions={0}, use_global_device_ids=true | all-gather | bytes 2560 | tf_op jit(solution)/shard_map/all_gather | solution.py:76
  54.7 1.3 fusion.46
  56.0 2.6 %collective-permute-start.3 = (bf16[4,256,512]{2,1,0:T(8,128)(2,1)S(1)}, bf16[4,256,512]{2,1,0:T(8,128)(2,1)S(1)}, u32[]{:S(2)}, u32[]{:S(2)}) collective-permute-start(bf16[4,256,512]{2,1,0:T(8,128)(2,1)S(1)} %get-tuple-element.40), channel_id=1, source_target_pairs={{0,4},{4,0},{8,12},{12,8},{16,20},{20,16},{24,28},{28,24},{32,36},... | collective-permute-start | bytes 3145736 | tf_op jit(solution)/shard_map/ppermute | solution.py:46
  58.7 19.3 %collective-permute-done.8 = bf16[4096,128]{0,1:T(8,128)(2,1)S(1)} collective-permute-done((bf16[4096,128]{0,1:T(8,128)(2,1)S(1)}, bf16[4096,128]{0,1:T(8,128)(2,1)S(1)}, u32[]{:S(2)}, u32[]{:S(2)}) %collective-permute-start.8) | collective-permute-done | bytes 1048608 | tf_op jit(solution)/shard_map/ppermute | solution.py:72
  78.6 0.3 maximum_select_fusion
  78.9 3.0 %copy-done.1 = bf16[8,4096,128]{1,2,0:T(8,128)(2,1)} copy-done((bf16[8,4096,128]{1,2,0:T(8,128)(2,1)}, bf16[8,4096,128]{1,2,0:T(8,128)(2,1)S(1)}, u32[]{:S(2)}) %copy-start.1) | copy-done | bytes 8388632
  81.9 1.5 rev.3
  83.4 2.3 %fusion.6 = bf16[4,512,512]{2,1,0:T(8,128)(2,1)S(1)} fusion(s32[]{:T(128)S(6)} %select_n.102, bf16[4,512,512]{2,1,0:T(8,128)(2,1)} %rev.3), kind=kLoop, calls=%fused_computation.37 | loop fusion | flops 1048576 | bytes 4194308 | tf_op jit(solution)/shard_map/concatenate | solution.py:83
  85.8 1.3 collective-permute-start.4
  87.1 2.5 %constant_dynamic-slice_fusion.2 = bf16[4,4096,128]{1,2,0:T(8,128)(2,1)S(1)} fusion(bf16[8,4096,128]{1,2,0:T(8,128)(2,1)} %copy-done.1, s32[]{:T(128)S(6)} %select_n.104), kind=kLoop, calls=%fused_computation.83 | loop fusion | bytes 8388612 | tf_op jit(solution)/shard_map/dynamic_slice | solution.py:74
  89.5 4.0 %collective-permute-start.5 = (bf16[8,512]{1,0:T(8,128)(2,1)S(1)}, bf16[8,512]{1,0:T(8,128)(2,1)S(1)}, u32[]{:S(2)}, u32[]{:S(2)}) collective-permute-start(bf16[8,512]{1,0:T(8,128)(2,1)S(1)} %get-tuple-element.31), channel_id=1, source_target_pairs={{0,32},{4,36},{8,40},{12,44},{16,48},{20,52},{24,56},{28,60},{32,6... | collective-permute-start | bytes 24584 | tf_op jit(solution)/shard_map/ppermute | solution.py:46
  93.5 1.6 maximum_dynamic-update-slice_fusion
  95.1 0.1 pad_maximum_fusion
  95.3 1.9 slice_dynamic-update-slice_fusion.6
  97.1 1.9 slice_dynamic-update-slice_fusion.5
  99.0 1.9 slice_dynamic-update-slice_fusion.4
  100.9 1.9 slice_dynamic-update-slice_fusion.3
  102.8 1.9 slice_dynamic-update-slice_fusion.2
  104.7 1.9 slice_dynamic-update-slice_fusion.1
  106.6 1.9 slice_dynamic-update-slice_fusion
  108.4 27.1 %multiply_add_fusion = f32[2048,1024]{1,0:T(8,128)S(1)} fusion(f32[1024]{0:T(1024)S(1)} %dynamic-slice-done, bf16[4096,2048]{1,0:T(8,128)(2,1)} %param.8, s32[]{:T(128)} %select_n.105, bf16[2056,4096]{1,0:T(8,128)(2,1)} %slice_dynamic-update-slice_fusion), kind=kOutput, calls=%fused_computation.3 | convolution fusion | flops 17217617920 | bytes 33559040 | tf_op jit(solution)/shard_map/dot_general | solution.py:93
  135.5 14.3 %multiply_add_fusion.1 = f32[2056,512]{1,0:T(8,128)S(1)} fusion(bf16[2056,4096]{1,0:T(8,128)(2,1)} %slice_dynamic-update-slice_fusion, bf16[4096,512]{0,1:T(8,128)(2,1)S(1)} %bitcast.87, f32[512]{0:T(512)S(1)} %bitcast.90), kind=kOutput, calls=%fused_computation.18 | convolution fusion | flops 8642437120 | bytes 25249792 | tf_op jit(solution)/shard_map/dot_general | solution.py:94
  149.8 2.4 %fusion.37 = f32[512,1024]{1,0:T(8,128)S(1)} fusion(f32[2056,512]{1,0:T(8,128)S(1)} %multiply_add_fusion.1, f32[2048,1024]{1,0:T(8,128)S(1)} %multiply_add_fusion), kind=kOutput, calls=%fused_computation.87 | convolution fusion | flops 2155872256 | bytes 12582912 | tf_op jit(solution)/shard_map/dot_general | solution.py:59
  152.1 2.4 %fusion.38 = f32[512,1024]{1,0:T(8,128)S(1)} fusion(f32[2056,512]{1,0:T(8,128)S(1)} %multiply_add_fusion.1, f32[2048,1024]{1,0:T(8,128)S(1)} %multiply_add_fusion), kind=kOutput, calls=%fused_computation.88 | convolution fusion | flops 2149580800 | bytes 12582912 | tf_op jit(solution)/shard_map/dot_general | solution.py:59
  154.5 2.6 %fusion.41 = f32[512,1024]{1,0:T(8,128)S(1)} fusion(f32[2048,1024]{1,0:T(8,128)S(1)} %multiply_add_fusion, f32[2056,512]{1,0:T(8,128)S(1)} %multiply_add_fusion.1, pred[2048]{0:T(1024)(128)(4,1)S(1)} %fusion.34), kind=kOutput, calls=%fused_computation.91 | convolution fusion | flops 2150629376 | bytes 12584960 | tf_op jit(solution)/shard_map/dot_general | solution.py:59
  157.1 2.7 %fusion.5 = f32[512,1024]{1,0:T(8,128)S(1)} fusion(f32[2056,512]{1,0:T(8,128)S(1)} %multiply_add_fusion.1, pred[2048]{0:T(1024)(128)(4,1)S(1)} %fusion.34, f32[2048,1024]{1,0:T(8,128)S(1)} %multiply_add_fusion), kind=kOutput, calls=%fused_computation.36 | convolution fusion | flops 2154823680 | bytes 16779264 | tf_op jit(solution)/shard_map/dot_general | solution.py:59
  159.7 2.4 %add_add_fusion.1 = f32[512,1024]{1,0:T(8,128)S(1)} fusion(f32[512,1024]{1,0:T(8,128)S(1)} %fusion.37, f32[512,1024]{1,0:T(8,128)S(1)} %fusion.38, f32[2056,512]{1,0:T(8,128)S(1)} %multiply_add_fusion.1, f32[2048,1024]{1,0:T(8,128)S(1)} %multiply_add_fusion), kind=kOutput, calls=%fused_computation.41 | convolution fusion | flops 2154823680 | bytes 18874368 | tf_op jit(solution)/shard_map/dot_general | solution.py:59
  162.1 2.6 %add_add_fusion = f32[512,1024]{1,0:T(8,128)S(1)} fusion(f32[512,1024]{1,0:T(8,128)S(1)} %fusion.41, f32[512,1024]{1,0:T(8,128)S(1)} %fusion.5, f32[2048,1024]{1,0:T(8,128)S(1)} %multiply_add_fusion, f32[2056,512]{1,0:T(8,128)S(1)} %multiply_add_fusion.1, pred[2048]{0:T(1024)(128)(4,1)S(1)} %fusion.34), kind=kOutput, calls=%fused_computation.39 | convolution fusion | flops 2157969408 | bytes 16779264 | tf_op jit(solution)/shard_map/dot_general | solution.py:59
  164.8 1.5 fusion.18
  166.3 1.0 slice_bitcast_fusion.1
  167.3 1.3 collective-permute-start.9
  168.6 1.4 collective-permute-start.11
  170.0 7.7 %collective-permute-done.9 = f32[128,1024]{1,0:T(8,128)} collective-permute-done((f32[128,1024]{1,0:T(8,128)}, f32[128,1024]{1,0:T(8,128)}, u32[]{:S(2)}, u32[]{:S(2)}) %collective-permute-start.9) | collective-permute-done | bytes 524320 | tf_op jit(solution)/shard_map/ppermute | solution.py:46
  177.7 2.3 %fusion.31 = (f32[2,128,1024]{2,1,0:T(8,128)S(1)}, f32[2,128,1024]{2,1,0:T(8,128)}) fusion(f32[2,128,1024]{2,1,0:T(8,128)S(1)} %get-tuple-element.28, f32[128,1024]{1,0:T(8,128)} %collective-permute-done.9, s32[]{:T(128)S(6)} %select_n.112, f32[1,4,128,1024]{3,2,1,0:T(8,128)S(1)} %bitcast.78, f32[1,4,128,1024]{3,2,1,0:T(8,128)} %bitcast.84, ...), kind=kLoop, calls=%fused_computation.71 | loop fusion | flops 524288 | bytes 6291464 | tf_op jit(solution)/shard_map/scatter-add | solution.py:111
  180.0 2.4 %collective-permute-start.12 = (f32[2,128,1024]{2,1,0:T(8,128)}, f32[2,128,1024]{2,1,0:T(8,128)}, u32[]{:S(2)}, u32[]{:S(2)}) collective-permute-start(f32[2,128,1024]{2,1,0:T(8,128)} %get-tuple-element.27), channel_id=1, source_target_pairs={{0,96},{4,100},{8,104},{12,108},{16,112},{20,116},{24,120},{28,124... | collective-permute-start | bytes 3145736 | tf_op jit(solution)/shard_map/ppermute | solution.py:46
  182.4 17.0 %collective-permute-done.12 = f32[2,128,1024]{2,1,0:T(8,128)} collective-permute-done((f32[2,128,1024]{2,1,0:T(8,128)}, f32[2,128,1024]{2,1,0:T(8,128)}, u32[]{:S(2)}, u32[]{:S(2)}) %collective-permute-start.12) | collective-permute-done | bytes 1048608 | tf_op jit(solution)/shard_map/ppermute | solution.py:46
  199.5 2.9 %collective-permute-done.10 = f32[2,128,1024]{2,1,0:T(8,128)} collective-permute-done((f32[2,128,1024]{2,1,0:T(8,128)S(1)}, f32[2,128,1024]{2,1,0:T(8,128)}, u32[]{:S(2)}, u32[]{:S(2)}) %collective-permute-start.10) | collective-permute-done | bytes 1048608 | tf_op jit(solution)/shard_map/ppermute | solution.py:46
  202.4 1.9 fusion.16
  204.4 7.0 %collective-permute-start.13 = (f32[2,64,1024]{2,1,0:T(8,128)S(1)}, f32[2,64,1024]{2,1,0:T(8,128)S(1)}, u32[]{:S(2)}, u32[]{:S(2)}) collective-permute-start(f32[2,64,1024]{2,1,0:T(8,128)S(1)} %get-tuple-element.36), channel_id=1, source_target_pairs={{0,4},{4,0},{8,12},{12,8},{16,20},{20,16},{24,28},{28,24},{32,36},... | collective-permute-start | bytes 1572872 | tf_op jit(solution)/shard_map/ppermute | solution.py:46
  211.4 1.5 collective-permute-done.13
  213.0 0.2 maximum_select_fusion.1
  213.2 1.1 fusion.32
  (33 shorter events, 1.0 us)
Async XLA Ops:
  0.6 5.3 %copy-start.2 = (bf16[256,512]{1,0:T(8,128)(2,1)S(1)}, bf16[256,512]{1,0:T(8,128)(2,1)}, u32[]{:S(2)}) copy-start(bf16[256,512]{1,0:T(8,128)(2,1)} %param.7) | copy-start | bytes 786436
  0.6 10.3 %copy-start.3 = (f32[2048]{0:T(1024)S(1)}, f32[2048]{0:T(1024)}, u32[]{:S(2)}) copy-start(f32[2048]{0:T(1024)} %param.9) | copy-start | bytes 24580
  2.6 56.0 %collective-permute-start.6 = (bf16[4096,128]{0,1:T(8,128)(2,1)S(1)}, bf16[4096,128]{0,1:T(8,128)(2,1)S(1)}, u32[]{:S(2)}, u32[]{:S(2)}) collective-permute-start(bf16[4096,128]{0,1:T(8,128)(2,1)S(1)} %copy.7), channel_id=1, source_target_pairs={{0,3},{1,0},{2,1},{3,2},{4,7},{5,4},{6,5},{7,6},{8,11},{9,8},{10,9... | collective-permute-start | bytes 3145736 | tf_op jit(solution)/shard_map/ppermute | solution.py:72
  5.9 48.6 %collective-permute-start.2 = (bf16[256,512]{1,0:T(8,128)(2,1)S(1)}, bf16[256,512]{1,0:T(8,128)(2,1)}, u32[]{:S(2)}, u32[]{:S(2)}) collective-permute-start(bf16[256,512]{1,0:T(8,128)(2,1)S(1)} %copy-done.2), channel_id=1, source_target_pairs={{0,24},{4,28},{8,0},{12,4},{16,8},{20,12},{24,16},{28,20},{32,56},... | collective-permute-start | bytes 786440 | tf_op jit(solution)/shard_map/ppermute | solution.py:46
  9.7 45.0 %collective-permute-start.1 = (bf16[256,512]{1,0:T(8,128)(2,1)S(1)}, bf16[256,512]{1,0:T(8,128)(2,1)}, u32[]{:S(2)}, u32[]{:S(2)}) collective-permute-start(bf16[256,512]{1,0:T(8,128)(2,1)S(1)} %copy-done.2), channel_id=1, source_target_pairs={{0,16},{4,20},{8,24},{12,28},{16,0},{20,4},{24,8},{28,12},{32,48},... | collective-permute-start | bytes 786440 | tf_op jit(solution)/shard_map/ppermute | solution.py:46
  9.7 45.0 %collective-permute-start = (bf16[256,512]{1,0:T(8,128)(2,1)S(1)}, bf16[256,512]{1,0:T(8,128)(2,1)}, u32[]{:S(2)}, u32[]{:S(2)}) collective-permute-start(bf16[256,512]{1,0:T(8,128)(2,1)S(1)} %copy-done.2), channel_id=1, source_target_pairs={{0,8},{4,12},{8,16},{12,20},{16,24},{20,28},{24,0},{28,4},{32,40},... | collective-permute-start | bytes 786440 | tf_op jit(solution)/shard_map/ppermute | solution.py:46
  10.4 48.2 %collective-permute-start.7 = (bf16[4096,128]{0,1:T(8,128)(2,1)S(1)}, bf16[4096,128]{0,1:T(8,128)(2,1)S(1)}, u32[]{:S(2)}, u32[]{:S(2)}) collective-permute-start(bf16[4096,128]{0,1:T(8,128)(2,1)S(1)} %copy.7), channel_id=1, source_target_pairs={{0,2},{1,3},{2,0},{3,1},{4,6},{5,7},{6,4},{7,5},{8,10},{9,11},{10,... | collective-permute-start | bytes 3145736 | tf_op jit(solution)/shard_map/ppermute | solution.py:72
  54.6 23.4 %collective-permute-start.8 = (bf16[4096,128]{0,1:T(8,128)(2,1)S(1)}, bf16[4096,128]{0,1:T(8,128)(2,1)S(1)}, u32[]{:S(2)}, u32[]{:S(2)}) collective-permute-start(bf16[4096,128]{0,1:T(8,128)(2,1)S(1)} %copy.7), channel_id=1, source_target_pairs={{0,1},{1,2},{2,3},{3,0},{4,5},{5,6},{6,7},{7,4},{8,9},{9,10},{10,1... | collective-permute-start | bytes 3145736 | tf_op jit(solution)/shard_map/ppermute | solution.py:72
  56.0 22.7 %collective-permute-start.3 = (bf16[4,256,512]{2,1,0:T(8,128)(2,1)S(1)}, bf16[4,256,512]{2,1,0:T(8,128)(2,1)S(1)}, u32[]{:S(2)}, u32[]{:S(2)}) collective-permute-start(bf16[4,256,512]{2,1,0:T(8,128)(2,1)S(1)} %get-tuple-element.40), channel_id=1, source_target_pairs={{0,4},{4,0},{8,12},{12,8},{16,20},{20,16},{24,28},{28,24},{32,36},... | collective-permute-start | bytes 3145736 | tf_op jit(solution)/shard_map/ppermute | solution.py:46
  78.6 3.3 %copy-start.1 = (bf16[8,4096,128]{1,2,0:T(8,128)(2,1)}, bf16[8,4096,128]{1,2,0:T(8,128)(2,1)S(1)}, u32[]{:S(2)}) copy-start(bf16[8,4096,128]{1,2,0:T(8,128)(2,1)S(1)} %bitcast_dynamic-update-slice_fusion.1) | copy-start | bytes 25165828
  85.8 7.8 %collective-permute-start.4 = (bf16[8,512]{1,0:T(8,128)(2,1)S(1)}, bf16[8,512]{1,0:T(8,128)(2,1)S(1)}, u32[]{:S(2)}, u32[]{:S(2)}) collective-permute-start(bf16[8,512]{1,0:T(8,128)(2,1)S(1)} %get-tuple-element.32), channel_id=1, source_target_pairs={{32,0},{36,4},{40,8},{44,12},{48,16},{52,20},{56,24},{60,28},{64,3... | collective-permute-start | bytes 24584 | tf_op jit(solution)/shard_map/ppermute | solution.py:46
  89.5 5.6 %collective-permute-start.5 = (bf16[8,512]{1,0:T(8,128)(2,1)S(1)}, bf16[8,512]{1,0:T(8,128)(2,1)S(1)}, u32[]{:S(2)}, u32[]{:S(2)}) collective-permute-start(bf16[8,512]{1,0:T(8,128)(2,1)S(1)} %get-tuple-element.31), channel_id=1, source_target_pairs={{0,32},{4,36},{8,40},{12,44},{16,48},{20,52},{24,56},{28,60},{32,6... | collective-permute-start | bytes 24584 | tf_op jit(solution)/shard_map/ppermute | solution.py:46
  104.7 3.8 %dynamic-slice-start = ((f32[2048]{0:T(1024)}, s32[]{:T(128)}), f32[1024]{0:T(1024)S(1)}, s32[]{:S(2)}) async-start(f32[2048]{0:T(1024)} %param.9, s32[]{:T(128)} %select_n.105), calls=%async_computation | async-start | bytes 8704 | tf_op jit(solution)/shard_map/dynamic_slice | solution.py:92
  164.7 2.6 %copy-start = (f32[512,1024]{1,0:T(8,128)}, f32[512,1024]{1,0:T(8,128)S(1)}, u32[]{:S(2)}) copy-start(f32[512,1024]{1,0:T(8,128)S(1)} %add_add_fusion) | copy-start | bytes 6291460
  167.3 10.4 %collective-permute-start.9 = (f32[128,1024]{1,0:T(8,128)}, f32[128,1024]{1,0:T(8,128)}, u32[]{:S(2)}, u32[]{:S(2)}) collective-permute-start(f32[128,1024]{1,0:T(8,128)} %get-tuple-element.37), channel_id=1, source_target_pairs={{0,32},{4,36},{8,40},{12,44},{16,48},{20,52},{24,56},{28,60},{32,6... | collective-permute-start | bytes 1572872 | tf_op jit(solution)/shard_map/ppermute | solution.py:46
  168.6 9.1 %collective-permute-start.11 = (f32[128,1024]{1,0:T(8,128)}, f32[128,1024]{1,0:T(8,128)}, u32[]{:S(2)}, u32[]{:S(2)}) collective-permute-start(f32[128,1024]{1,0:T(8,128)} %get-tuple-element.38), channel_id=1, source_target_pairs={{0,96},{4,100},{8,104},{12,108},{16,112},{20,116},{24,120},{28,124... | collective-permute-start | bytes 1572872 | tf_op jit(solution)/shard_map/ppermute | solution.py:46
  180.0 19.4 %collective-permute-start.12 = (f32[2,128,1024]{2,1,0:T(8,128)}, f32[2,128,1024]{2,1,0:T(8,128)}, u32[]{:S(2)}, u32[]{:S(2)}) collective-permute-start(f32[2,128,1024]{2,1,0:T(8,128)} %get-tuple-element.27), channel_id=1, source_target_pairs={{0,96},{4,100},{8,104},{12,108},{16,112},{20,116},{24,120},{28,124... | collective-permute-start | bytes 3145736 | tf_op jit(solution)/shard_map/ppermute | solution.py:46
  182.4 19.9 %collective-permute-start.10 = (f32[2,128,1024]{2,1,0:T(8,128)S(1)}, f32[2,128,1024]{2,1,0:T(8,128)}, u32[]{:S(2)}, u32[]{:S(2)}) collective-permute-start(f32[2,128,1024]{2,1,0:T(8,128)S(1)} %get-tuple-element.26), channel_id=1, source_target_pairs={{0,32},{4,36},{8,40},{12,44},{16,48},{20,52},{24,56},{28,60},{32,6... | collective-permute-start | bytes 3145736 | tf_op jit(solution)/shard_map/ppermute | solution.py:46
  204.4 8.6 %collective-permute-start.13 = (f32[2,64,1024]{2,1,0:T(8,128)S(1)}, f32[2,64,1024]{2,1,0:T(8,128)S(1)}, u32[]{:S(2)}, u32[]{:S(2)}) collective-permute-start(f32[2,64,1024]{2,1,0:T(8,128)S(1)} %get-tuple-element.36), channel_id=1, source_target_pairs={{0,4},{4,0},{8,12},{12,8},{16,20},{20,16},{24,28},{28,24},{32,36},... | collective-permute-start | bytes 1572872 | tf_op jit(solution)/shard_map/ppermute | solution.py:46

commit v2 on v1

v2 whole, which is shorter than its diff:
```python
import functools
import math

import jax
import jax.numpy as jnp
import numpy as np
from jax import lax
from jax.experimental import pallas as pl
from jax.experimental.pallas import tpu as pltpu
from jax.sharding import PartitionSpec as P

CWD = 512
Y, Z, C = 4, 4, 2
LAGS = 8
BLOCK = 256
CHUNKS = 2

TWO_PI_HIGH = 6.28125
TWO_PI_LOW = 2 * math.pi - TWO_PI_HIGH


def half_cos_terms():
    fit = np.polynomial.chebyshev.Chebyshev.interpolate(
        lambda q: np.cos(np.sqrt(q) / 2), 4, domain=[0.0, (math.pi * 1.0005) ** 2]
    )
    return [float(v * math.sqrt(2 * math.sqrt(2.0))) for v in fit.convert(kind=np.polynomial.Polynomial).coef]


TERMS = half_cos_terms()


def feature(angle):
    turns = jnp.round(angle * (1 / (2 * math.pi)))
    rest = (angle - turns * TWO_PI_HIGH) - turns * TWO_PI_LOW
    q = rest * rest
    p = TERMS[4]
    for term in TERMS[3::-1]:
        p = p * q + term
    return p * p - math.sqrt(2.0)


def split(value):
    high = value.astype(jnp.bfloat16)
    return high, (value - high.astype(jnp.float32)).astype(jnp.bfloat16)


def move(value, to):
    pairs = []
    for y in range(Y):
        for z in range(Z):
            for c in range(C):
                goal = to(y, z, c)
                if goal is not None:
                    gy, gz, gc = goal
                    pairs.append(((y * Z + z) * C + c, (gy % Y * Z + gz % Z) * C + gc % C))
    return lax.ppermute(value, "tm", pairs)


def swap(value):
    return move(value, lambda y, z, c: (y, z, 1 - c))


def around(value, by):
    return lax.ppermute(value, "feat", [(i, (i + by) % 4) for i in range(4)])


def lay_out(x_ref, edge_ref, lagged):
    rows = x_ref.shape[1]
    at = lax.broadcasted_iota(jnp.int32, x_ref.shape[1:], 0)
    for i in range(LAGS):
        lagged[7 + i] = x_ref[i]
    for i in range(1, LAGS):
        older = pltpu.roll(x_ref[i].astype(jnp.float32), 1, 0)
        edge = edge_ref[0, i : i + 1].astype(jnp.float32)
        lagged[i - 1] = jnp.where(at == 0, edge, older).astype(jnp.bfloat16)
    newer = pltpu.roll(x_ref[0].astype(jnp.float32), rows - 1, 0)
    edge = edge_ref[1, 0:1].astype(jnp.float32)
    lagged[15] = jnp.where(at == rows - 1, edge, newer).astype(jnp.bfloat16)


def feats_kernel(place, x_ref, edge_ref, p_ref, shift_ref, high_ref, low_ref, lagged):
    @pl.when(pl.program_id(0) == 0)
    def _():
        lay_out(x_ref, edge_ref, lagged)

    rows = x_ref.shape[1]
    for i in range(LAGS):
        left = jnp.concatenate([lagged[7 + i - k] for k in range(LAGS)], 1)
        angle = jnp.dot(left, p_ref[...], preferred_element_type=jnp.float32) + shift_ref[...]
        high, low = split(feature(angle))
        high_ref[i * rows : (i + 1) * rows, :] = high
        low_ref[i * rows : (i + 1) * rows, :] = low


def feats_of(place, x, edge, projection, shift):
    rows, pcs = x.shape[1:]
    depth, width = projection.shape
    half = width // C
    blocks = half // BLOCK
    out = jax.ShapeDtypeStruct((LAGS * rows, half), jnp.bfloat16)
    return pl.pallas_call(
        feats_kernel,
        out_shape=(out, out),
        grid_spec=pltpu.PrefetchScalarGridSpec(
            num_scalar_prefetch=1,
            grid=(blocks,),
            in_specs=[
                pl.BlockSpec(x.shape, lambda n, s: (0, 0, 0)),
                pl.BlockSpec(edge.shape, lambda n, s: (0, 0, 0)),
                pl.BlockSpec((depth, BLOCK), lambda n, s: (0, s[2] * blocks + n)),
                pl.BlockSpec((1, BLOCK), lambda n, s: (0, s[2] * blocks + n)),
            ],
            out_specs=[pl.BlockSpec((LAGS * rows, BLOCK), lambda n, s: (0, n))] * 2,
            scratch_shapes=[pltpu.VMEM((16, rows, pcs), jnp.bfloat16)],
        ),
        compiler_params=pltpu.CompilerParams(vmem_limit_bytes=40 << 20),
        cost_estimate=pl.CostEstimate(
            flops=2 * LAGS * rows * depth * half, bytes_accessed=2 * depth * half, transcendentals=0
        ),
        name="feats",
    )(place, x, edge, projection, shift)


def window_kernel(place, x_ref, edge_ref, mine_ref, near_ref, swapped_ref, shift_ref, high_ref, low_ref, lagged):
    lay_out(x_ref, edge_ref, lagged)
    rows = x_ref.shape[1]
    y, c = place[0], place[2]
    depth = near_ref.shape[1]
    lags = depth // x_ref.shape[2]
    sides = []
    for own, ref in ((c, near_ref), (1 - c, swapped_ref)):
        mine = mine_ref[pl.ds(pl.multiple_of(own * depth, depth), depth), :]
        sides.append((own * lags, jnp.concatenate([mine, ref[0], ref[1], ref[2]], 1)))
    at = lax.broadcasted_iota(jnp.int32, (rows, 1), 0)
    for i in range(LAGS + 1):
        angle = shift_ref[...]
        for first, right in sides:
            left = jnp.concatenate([lagged[7 + i - k - first] for k in range(lags)], 1)
            angle = angle + jnp.dot(left, right, preferred_element_type=jnp.float32)
        value = feature(angle)
        if i == LAGS:
            value = jnp.where((at == rows - 1) & (y == Y - 1), 0.0, value)
        high, low = split(value.T)
        high_ref[:, i * rows : (i + 1) * rows] = high
        low_ref[:, i * rows : (i + 1) * rows] = low


def window_of(place, x, edge, mine, near, swapped, shift):
    rows, pcs = x.shape[1:]
    out = jax.ShapeDtypeStruct((CWD, (LAGS + 1) * rows), jnp.bfloat16)
    return pl.pallas_call(
        window_kernel,
        out_shape=(out, out),
        in_specs=[pl.BlockSpec(memory_space=pltpu.SMEM)] + [pl.BlockSpec(memory_space=pltpu.VMEM)] * 6,
        out_specs=[pl.BlockSpec(memory_space=pltpu.VMEM)] * 2,
        scratch_shapes=[pltpu.VMEM((16, rows, pcs), jnp.bfloat16)],
        compiler_params=pltpu.CompilerParams(vmem_limit_bytes=40 << 20),
        cost_estimate=pl.CostEstimate(
            flops=2 * (LAGS + 1) * rows * LAGS * pcs * CWD, bytes_accessed=2 * LAGS * pcs * CWD, transcendentals=0
        ),
        name="window",
    )(place, x, edge, mine, near, swapped, shift)


def products_kernel(rows, wh_ref, wl_ref, fh_ref, fl_ref, out_ref):
    count = fh_ref.shape[0]
    for which in range(2):
        span = slice(which * rows, which * rows + count)
        total = jnp.dot(wh_ref[:, span], fh_ref[...], preferred_element_type=jnp.float32)
        total += jnp.dot(wl_ref[:, span], fh_ref[...], preferred_element_type=jnp.float32)
        total += jnp.dot(wh_ref[:, span], fl_ref[...], preferred_element_type=jnp.float32)
        out_ref[which] = total


def products_of(chunk, wh, wl, fh, fl):
    count, half = fh.shape
    width = half // CHUNKS
    steps = width // BLOCK
    return pl.pallas_call(
        functools.partial(products_kernel, wh.shape[1] - count),
        out_shape=jax.ShapeDtypeStruct((2, CWD, width), jnp.float32),
        grid=(steps,),
        in_specs=[pl.BlockSpec(wh.shape, lambda n: (0, 0))] * 2
        + [pl.BlockSpec((count, BLOCK), lambda n: (0, chunk * steps + n))] * 2,
        out_specs=pl.BlockSpec((2, CWD, BLOCK), lambda n: (0, 0, n)),
        compiler_params=pltpu.CompilerParams(vmem_limit_bytes=40 << 20),
        cost_estimate=pl.CostEstimate(flops=12 * count * CWD * width, bytes_accessed=8 << 20, transcendentals=0),
        name="products",
    )(wh, wl, fh, fl)


def local(snapshots, projection, phase_shift):
    rows, pcs = snapshots.shape
    position = lax.axis_index("tm")
    y, z, c = position // (Z * C), position // C % Z, position % C
    x = lax.axis_index("feat")
    place = jnp.stack([y, z, c])

    width = CWD // Z
    depth = projection.shape[0]
    mine = lax.dynamic_slice_in_dim(projection, z * width, width, 1)
    piece = lax.dynamic_slice_in_dim(mine, c * (depth // C), depth // C, 0)
    near = jnp.stack([around(piece, by) for by in (1, 2, 3)])
    swapped = swap(near)
    shift = lax.dynamic_slice_in_dim(phase_shift, z * width, width, 0)[None]
    shifts = jnp.concatenate([shift] + [around(shift, by) for by in (1, 2, 3)], 1)

    phased = jnp.swapaxes(snapshots.reshape(rows // LAGS, LAGS, pcs), 0, 1)
    own = jnp.stack([phased] + [move(phased, lambda y, z, c, by=by: (y, z + by, c)) for by in (1, 2, 3)])
    other = swap(own)
    pair = jnp.where(c == 0, jnp.stack([own, other], 1), jnp.stack([other, own], 1))[::-1]
    slab = lax.dynamic_slice_in_dim(jnp.concatenate([pair, pair]), 3 - z, 4, 0)
    slab = jnp.moveaxis(slab.reshape(Z * C, LAGS, rows // LAGS, pcs), 0, 1).reshape(LAGS, -1, pcs)
    before = move(slab[:, -1], lambda y, z, c: (y + 1, z, c) if y < Y - 1 else None)
    after = move(slab[:, 0], lambda y, z, c: (y - 1, z, c) if y > 0 else None)
    edge = jnp.stack([before, after])

    fh, fl = feats_of(place, slab, edge, projection, phase_shift[None])
    wh, wl = window_of(place, slab, edge, mine, near, swapped, shifts)

    def summed(chunk):
        both = products_of(chunk, wh, wl, fh, fl)

        def toward(by):
            slot = (x - y - by) % 4
            return lax.dynamic_slice_in_dim(both, slot * width, width, 1)

        far = toward(2)
        up = move(far[0], lambda y, z, c: (y + 1, z, c))
        down = move(far[1], lambda y, z, c: (y - 1, z, c))
        from_below = move(toward(1).at[0].add(up), lambda y, z, c: (y + 1, z, c))
        from_above = move(toward(3).at[1].add(down), lambda y, z, c: (y - 1, z, c))
        return toward(0) + from_below + from_above

    total = jnp.concatenate([summed(chunk) for chunk in range(CHUNKS)], 2)

    part = width // C
    theirs = swap(lax.dynamic_slice_in_dim(total, (1 - c) * part, part, 1))
    ours = lax.dynamic_slice_in_dim(total, c * part, part, 1)
    whole = jnp.where(c == 0, jnp.concatenate([ours, theirs], 2), jnp.concatenate([theirs, ours], 2))
    steps = rows * Y * Z * C
    return whole[0].T / steps, whole[1].T / (steps - 1)


def solution(mesh):
    in_specs = (P("tm", None), P(None, "feat"), P("feat"))
    out_specs = (P("feat", "tm"), P("feat", "tm"))
    return jax.shard_map(local, mesh=mesh, in_specs=in_specs, out_specs=out_specs, check_vma=False)
```

time: 215 us -> 162 us (0.75)
  Pallas kernels: 0 us -> 56.4 us
  matrix products: 56.3 us -> 0 us
  blocking collectives: 43.6 us -> 0 us
  local copies, waits for them, and re-layouts: 23.9 us -> 10.3 us
  starting transfers between devices: 28.4 us -> 33.3 us
    pallas_call x0 -> x4, Pallas kernels: none -> 56.4 us  [the longest x1 26.3 us: feats_of(): pl.pallas_call(feats_kernel, out_shape=(out, out), grid_spec=pltpu.Prefet...]
    dot_general x8 -> x0, matrix products: 56.3 us -> none  [the longest x1 27.1 us: local(): jnp.dot(embedded[:count], own_projection, preferred_element_type=jnp.floa...]
    all_gather x1 -> x0, blocking collectives: 43.6 us -> none  [local(): lax.all_gather(lax.dynamic_slice_in_dim(phase_shift, z * width, width, 0)...]
    unnamed x23 -> x6, local copies, waits for them, and re-layouts: 15.5 us -> 1.96 us
    ppermute x3 -> x6, waiting for transfers between devices: 19.3 us -> 14.4 us  [around(): return lax.ppermute(value, 'feat', [(i, (i + by) % 4) for i in range(4)])]
    ppermute x3 -> x6, starting transfers between devices: 3.97 us -> 7 us  [around(): return lax.ppermute(value, 'feat', [(i, (i + by) % 4) for i in range(4)])]
    ppermute x11 -> x16, waiting for transfers between devices: 29.2 us -> 32.1 us  [move(): return lax.ppermute(value, 'tm', pairs)]
    select_n x1, other arithmetic: 0.29 us -> 2.59 us  [local(): jnp.where(c == 0, jnp.stack([own, other], 1), jnp.stack([other, own], 1))]
  transfers between devices with their start and end apart: 14 -> 22, of which waited for: 5 -> 9; matrix products, arithmetic and copies ran while one was open for 3% -> 11% of each run, Pallas kernels for 0% -> 16%
where the time goes in v2:
time: 162 us
  Pallas kernels  56.4 us (35%)
  waiting for transfers between devices  46.5 us (29%)
  starting transfers between devices  33.3 us (21%)
  other arithmetic  14.3 us (9%)
  local copies, waits for them, and re-layouts  10.3 us (6%)
    ppermute x16, waiting for transfers between devices, move(): return lax.ppermute(value, 'tm', pairs)  32.1 us
    pallas_call x1, Pallas kernels, feats_of(): pl.pallas_call(feats_kernel, out_shape=(out, out), grid_spec=pltpu.Prefet...  26.3 us
    ppermute x16, starting transfers between devices, move(): return lax.ppermute(value, 'tm', pairs)  26.3 us
    pallas_call x2, Pallas kernels, products_of(): pl.pallas_call(functools.partial(products_kernel, wh.shape[1] - count), o...  17 us
    ppermute x6, waiting for transfers between devices, around(): return lax.ppermute(value, 'feat', [(i, (i + by) % 4) for i in range(4)])  14.4 us
    pallas_call x1, Pallas kernels, window_of(): pl.pallas_call(window_kernel, out_shape=(out, out), in_specs=[pl.BlockSpe...  13 us
    ppermute x6, starting transfers between devices, around(): return lax.ppermute(value, 'feat', [(i, (i + by) % 4) for i in range(4)])  7 us
  transfers between devices with their start and end apart: 22, of which 9 were waited for; matrix products, arithmetic and copies ran while one was open for 11% of the time, Pallas kernels for 16%

profile of v2, /device:TPU:1, one launch (start us, length us, event | category | flops | bytes accessed | tf_op | source)
XLA Modules:
  0.0 161.6 jit_solution(3597646386998718700)
XLA Ops:
  0.6 4.5 %collective-permute-start.1 = (bf16[8,32,512]{2,0,1:T(8,128)(2,1)}, bf16[8,32,512]{2,0,1:T(8,128)(2,1)S(1)}, u32[]{:S(2)}, u32[]{:S(2)}) collective-permute-start(bf16[8,32,512]{2,0,1:T(8,128)(2,1)} %bitcast.66), channel_id=1, source_target_pairs={{0,16},{4,20},{8,24},{12,28},{16,0},{20,4},{24,8},{28,12},{32,48},... | collective-permute-start | bytes 786440 | tf_op jit(solution)/shard_map/ppermute | solution.py:56
  5.1 0.7 collective-permute-start
  5.9 1.9 %collective-permute-start.2 = (bf16[8,32,512]{2,0,1:T(8,128)(2,1)}, bf16[8,32,512]{2,0,1:T(8,128)(2,1)S(1)}, u32[]{:S(2)}, u32[]{:S(2)}) collective-permute-start(bf16[8,32,512]{2,0,1:T(8,128)(2,1)} %bitcast.68), channel_id=1, source_target_pairs={{0,24},{4,28},{8,0},{12,4},{16,8},{20,12},{24,16},{28,20},{32,56},... | collective-permute-start | bytes 786440 | tf_op jit(solution)/shard_map/ppermute | solution.py:56
  7.8 3.6 %collective-permute-done.1 = bf16[8,32,512]{2,0,1:T(8,128)(2,1)S(1)} collective-permute-done((bf16[8,32,512]{2,0,1:T(8,128)(2,1)}, bf16[8,32,512]{2,0,1:T(8,128)(2,1)S(1)}, u32[]{:S(2)}, u32[]{:S(2)}) %collective-permute-start.1) | collective-permute-done | bytes 262176 | tf_op jit(solution)/shard_map/ppermute | solution.py:56
  11.4 6.3 %collective-permute-done = bf16[8,32,512]{2,0,1:T(8,128)(2,1)S(1)} collective-permute-done((bf16[8,32,512]{2,0,1:T(8,128)(2,1)}, bf16[8,32,512]{2,0,1:T(8,128)(2,1)S(1)}, u32[]{:S(2)}, u32[]{:S(2)}) %collective-permute-start) | collective-permute-done | bytes 262176 | tf_op jit(solution)/shard_map/ppermute | solution.py:56
  17.7 2.1 %fusion.9 = (bf16[4,1,8,32,512]{4,2,3,0,1:T(8,128)(2,1)}, bf16[4,8,32,512]{3,1,2,0:T(8,128)(2,1)S(1)}) fusion(bf16[1,8,32,512]{3,1,2,0:T(8,128)(2,1)S(1)} %bitcast.72, bf16[1,8,32,512]{3,1,2,0:T(8,128)(2,1)S(1)} %bitcast.70, bf16[1,8,32,512]{3,1,2,0:T(8,128)(2,1)S(1)} %bitcast.71, bf16[1,8,32,512]{3,1,2,0:T(8,128)(2,1)} %bitcast.69), kind=kLoop, calls=%fused_computation.42 | loop fusion | flops 1572864 | bytes 3145728 | tf_op jit(solution)/shard_map/stack | solution.py:211
  19.8 1.3 collective-permute-start.3
  21.2 2.5 %collective-permute-start.12 = (f32[1,128]{1,0:T(1,128)S(1)}, f32[1,128]{1,0:T(1,128)S(1)}, u32[]{:S(2)}, u32[]{:S(2)}) collective-permute-start(f32[1,128]{1,0:T(1,128)S(1)} %dynamic-slice_bitcast_fusion.4), channel_id=1, source_target_pairs={{0,3},{1,0},{2,1},{3,2},{4,7},{5,4},{6,5},{7,6},{8,11},{9,8},{10,9... | collective-permute-start | bytes 1544 | tf_op jit(solution)/shard_map/ppermute | solution.py:64
  24.2 0.6 collective-permute-start.10
  24.8 2.4 %dynamic_slice.44 = bf16[2048,128]{1,0:T(8,128)(2,1)} dynamic-slice(bf16[4096,2048]{1,0:T(8,128)(2,1)} %p_ref.1, s32[]{:T(128)S(6)} %select_n.108, s32[]{:T(128)S(6)} %select_n.109), dynamic_slice_sizes={2048,128} | dynamic-slice | bytes 1048580 | tf_op jit(solution)/shard_map/dynamic_slice | solution.py:202
  27.2 2.1 %collective-permute-start.8 = (bf16[2048,128]{1,0:T(8,128)(2,1)}, bf16[2048,128]{1,0:T(8,128)(2,1)}, u32[]{:S(2)}, u32[]{:S(2)}) collective-permute-start(bf16[2048,128]{1,0:T(8,128)(2,1)} %dynamic_slice.44), channel_id=1, source_target_pairs={{0,3},{1,0},{2,1},{3,2},{4,7},{5,4},{6,5},{7,6},{8,11},{9,8},{10,9... | collective-permute-start | bytes 1572872 | tf_op jit(solution)/shard_map/ppermute | solution.py:64
  29.3 1.3 constant_dynamic-slice_fusion.4.mine_ref
  30.7 1.3 collective-permute-start.7
  32.0 2.6 %maximum_select_fusion = bf16[4,2,8,32,512]{4,2,3,0,1:T(8,128)(2,1)S(1)} fusion(bf16[4,1,8,32,512]{4,2,3,0,1:T(8,128)(2,1)} %bitcast.11, bf16[4,1,8,32,512]{4,2,3,0,1:T(8,128)(2,1)} %get-tuple-element.76, pred[]{:T(512)S(6)} %eq.15), kind=kLoop, calls=%fused_computation.3 | loop fusion | flops 3145728 | bytes 4194305 | tf_op jit(solution)/shard_map/jit(_where)/select_n | solution.py:211
  34.6 1.6 rev.3
  36.2 2.3 %fusion = bf16[4,2,8,32,512]{4,2,3,0,1:T(8,128)(2,1)S(1)} fusion(s32[]{:T(128)S(6)} %select_n.105, bf16[4,2,8,32,512]{4,2,3,0,1:T(8,128)(2,1)} %rev.3), kind=kLoop, calls=%fused_computation.2 | loop fusion | flops 1048576 | bytes 4194308 | tf_op jit(solution)/shard_map/concatenate | solution.py:212
  38.7 3.2 %collective-permute-start.4 = (bf16[8,512]{1,0:T(8,128)(2,1)S(1)}, bf16[8,512]{1,0:T(8,128)(2,1)S(1)}, u32[]{:S(2)}, u32[]{:S(2)}) collective-permute-start(bf16[8,512]{1,0:T(8,128)(2,1)S(1)} %get-tuple-element.70), channel_id=1, source_target_pairs={{0,32},{4,36},{8,40},{12,44},{16,48},{20,52},{24,56},{28,60},{32,6... | collective-permute-start | bytes 24584 | tf_op jit(solution)/shard_map/ppermute | solution.py:56
  41.9 1.3 collective-permute-start.5
  43.3 1.6 %collective-permute-done.7 = bf16[2048,128]{1,0:T(8,128)(2,1)} collective-permute-done((bf16[2048,128]{1,0:T(8,128)(2,1)}, bf16[2048,128]{1,0:T(8,128)(2,1)}, u32[]{:S(2)}, u32[]{:S(2)}) %collective-permute-start.7) | collective-permute-done | bytes 524320 | tf_op jit(solution)/shard_map/ppermute | solution.py:64
  44.9 12.7 %collective-permute-done.6 = bf16[2048,128]{1,0:T(8,128)(2,1)} collective-permute-done((bf16[2048,128]{1,0:T(8,128)(2,1)}, bf16[2048,128]{1,0:T(8,128)(2,1)}, u32[]{:S(2)}, u32[]{:S(2)}) %collective-permute-start.6) | collective-permute-done | bytes 524320 | tf_op jit(solution)/shard_map/ppermute | solution.py:64
  57.6 1.5 pad_maximum_fusion.near_ref
  59.2 0.8 collective-permute-start.9
  59.9 0.7 copy.6.x_ref
  60.6 26.3 %feats.1 = (bf16[2048,1024]{1,0:T(8,128)(2,1)S(1)}, bf16[2048,1024]{1,0:T(8,128)(2,1)S(1)}) custom-call(s32[3]{0:T(128)S(1)} %pad_add_fusion.place, bf16[8,256,512]{2,1,0:T(8,128)(2,1)S(1)} %copy.6.x_ref, bf16[2,8,512]{2,1,0:T(8,128)(2,1)S(1)} %pad_maximum_fusion.2.edge_ref, bf16[4096,2048]{1,0:T(8,128)(2,1)} %p_ref.1, f32[1,2048]{1,0:T(1,128)S(1)} %bitcast.63), custom_call_target="tpu_custom_call" | custom-call | flops 17179869184 | bytes 8388608 | tf_op jit(solution)/shard_map/feats/pallas_call | solution.py:101
  87.0 2.0 %copy-done.2 = bf16[2048,1024]{1,0:T(8,128)(2,1)} copy-done((bf16[2048,1024]{1,0:T(8,128)(2,1)}, bf16[2048,1024]{1,0:T(8,128)(2,1)S(1)}, u32[]{:S(2)}) %copy-start.2) | copy-done | bytes 4194328
  88.9 13.0 %window.1 = (bf16[512,2304]{1,0:T(8,128)(2,1)S(1)}, bf16[512,2304]{1,0:T(8,128)(2,1)S(1)}) custom-call(s32[3]{0:T(128)S(1)} %pad_add_fusion.place, bf16[8,256,512]{2,1,0:T(8,128)(2,1)S(1)} %copy.6.x_ref, bf16[2,8,512]{2,1,0:T(8,128)(2,1)S(1)} %pad_maximum_fusion.2.edge_ref, bf16[4096,128]{1,0:T(8,128)(2,1)S(1)} %constant_dynamic-slice_fusion.4.mine_ref, ...), custom_call_target="tpu_custom_call" | custom-call | flops 9663676416 | bytes 4194304 | tf_op jit(solution)/shard_map/window/pallas_call | solution.py:151
  102.0 8.4 %products.3 = f32[2,512,512]{2,1,0:T(8,128)S(1)} custom-call(bf16[512,2304]{1,0:T(8,128)(2,1)S(1)} %get-tuple-element.54.wh_ref, bf16[512,2304]{1,0:T(8,128)(2,1)S(1)} %get-tuple-element.55.wl_ref, bf16[2048,1024]{1,0:T(8,128)(2,1)S(1)} %get-tuple-element.56.fh_ref, bf16[2048,1024]{1,0:T(8,128)(2,1)} %copy-done.2), custom_call_target="tpu_custom_call" | custom-call | flops 6442450944 | bytes 8388608 | tf_op jit(solution)/shard_map/products/pallas_call | solution.py:179
  110.4 8.6 %products.2 = f32[2,512,512]{2,1,0:T(8,128)S(1)} custom-call(bf16[512,2304]{1,0:T(8,128)(2,1)S(1)} %get-tuple-element.54.wh_ref, bf16[512,2304]{1,0:T(8,128)(2,1)S(1)} %get-tuple-element.55.wl_ref, bf16[2048,1024]{1,0:T(8,128)(2,1)S(1)} %get-tuple-element.56.fh_ref, bf16[2048,1024]{1,0:T(8,128)(2,1)} %copy-done.2), custom_call_target="tpu_custom_call" | custom-call | flops 6442450944 | bytes 8388608 | tf_op jit(solution)/shard_map/products/pallas_call | solution.py:179
  119.0 1.3 collective-permute-start.13
  120.4 1.5 collective-permute-start.15
  122.0 2.7 %collective-permute-start.19 = (f32[128,512]{1,0:T(8,128)S(1)}, f32[128,512]{1,0:T(8,128)S(1)}, u32[]{:S(2)}, u32[]{:S(2)}) collective-permute-start(f32[128,512]{1,0:T(8,128)S(1)} %get-tuple-element.61), channel_id=1, source_target_pairs={{0,96},{4,100},{8,104},{12,108},{16,112},{20,116},{24,120},{28,124... | collective-permute-start | bytes 786440 | tf_op jit(solution)/shard_map/ppermute | solution.py:56
  124.7 1.0 constant_dynamic-slice_fusion.3
  125.7 2.6 %collective-permute-done.13 = f32[128,512]{1,0:T(8,128)S(1)} collective-permute-done((f32[128,512]{1,0:T(8,128)S(1)}, f32[128,512]{1,0:T(8,128)S(1)}, u32[]{:S(2)}, u32[]{:S(2)}) %collective-permute-start.13) | collective-permute-done | bytes 262176 | tf_op jit(solution)/shard_map/ppermute | solution.py:56
  128.3 0.9 fusion.8
  129.2 0.9 collective-permute-start.14
  130.1 1.8 %collective-permute-start.16 = (f32[2,128,512]{2,1,0:T(8,128)}, f32[2,128,512]{2,1,0:T(8,128)S(1)}, u32[]{:S(2)}, u32[]{:S(2)}) collective-permute-start(f32[2,128,512]{2,1,0:T(8,128)} %get-tuple-element.65), channel_id=1, source_target_pairs={{0,96},{4,100},{8,104},{12,108},{16,112},{20,116},{24,120},{28,124... | collective-permute-start | bytes 1572872 | tf_op jit(solution)/shard_map/ppermute | solution.py:56
  131.9 1.0 constant_dynamic-slice_fusion.1
  133.0 1.0 collective-permute-done.17
  134.0 0.9 fusion.6
  134.9 0.9 collective-permute-start.18
  135.8 1.8 %collective-permute-start.20 = (f32[2,128,512]{2,1,0:T(8,128)}, f32[2,128,512]{2,1,0:T(8,128)}, u32[]{:S(2)}, u32[]{:S(2)}) collective-permute-start(f32[2,128,512]{2,1,0:T(8,128)} %get-tuple-element.59), channel_id=1, source_target_pairs={{0,96},{4,100},{8,104},{12,108},{16,112},{20,116},{24,120},{28,124... | collective-permute-start | bytes 1572872 | tf_op jit(solution)/shard_map/ppermute | solution.py:56
  137.5 6.9 %collective-permute-done.14 = f32[2,128,512]{2,1,0:T(8,128)S(1)} collective-permute-done((f32[2,128,512]{2,1,0:T(8,128)}, f32[2,128,512]{2,1,0:T(8,128)S(1)}, u32[]{:S(2)}, u32[]{:S(2)}) %collective-permute-start.14) | collective-permute-done | bytes 524320 | tf_op jit(solution)/shard_map/ppermute | solution.py:56
  144.4 1.2 add_add_fusion.1
  145.6 10.1 %collective-permute-done.18 = f32[2,128,512]{2,1,0:T(8,128)} collective-permute-done((f32[2,128,512]{2,1,0:T(8,128)}, f32[2,128,512]{2,1,0:T(8,128)}, u32[]{:S(2)}, u32[]{:S(2)}) %collective-permute-start.18) | collective-permute-done | bytes 524320 | tf_op jit(solution)/shard_map/ppermute | solution.py:56
  155.8 1.4 add_add_fusion
  157.2 1.6 collective-permute-start.21
  158.8 1.5 collective-permute-done.21
  160.6 1.1 fusion.3
  (31 shorter events, 1.4 us)
Async XLA Ops:
  0.6 20.5 %copy-start.1 = (f32[2048]{0:T(1024)S(1)}, f32[2048]{0:T(1024)}, u32[]{:S(2)}) copy-start(f32[2048]{0:T(1024)} %param.13) | copy-start | bytes 24580
  0.6 10.8 %collective-permute-start.1 = (bf16[8,32,512]{2,0,1:T(8,128)(2,1)}, bf16[8,32,512]{2,0,1:T(8,128)(2,1)S(1)}, u32[]{:S(2)}, u32[]{:S(2)}) collective-permute-start(bf16[8,32,512]{2,0,1:T(8,128)(2,1)} %bitcast.66), channel_id=1, source_target_pairs={{0,16},{4,20},{8,24},{12,28},{16,0},{20,4},{24,8},{28,12},{32,48},... | collective-permute-start | bytes 786440 | tf_op jit(solution)/shard_map/ppermute | solution.py:56
  5.1 12.6 %collective-permute-start = (bf16[8,32,512]{2,0,1:T(8,128)(2,1)}, bf16[8,32,512]{2,0,1:T(8,128)(2,1)S(1)}, u32[]{:S(2)}, u32[]{:S(2)}) collective-permute-start(bf16[8,32,512]{2,0,1:T(8,128)(2,1)} %bitcast.67), channel_id=1, source_target_pairs={{0,8},{4,12},{8,16},{12,20},{16,24},{20,28},{24,0},{28,4},{32,40},... | collective-permute-start | bytes 786440 | tf_op jit(solution)/shard_map/ppermute | solution.py:56
  5.9 11.9 %collective-permute-start.2 = (bf16[8,32,512]{2,0,1:T(8,128)(2,1)}, bf16[8,32,512]{2,0,1:T(8,128)(2,1)S(1)}, u32[]{:S(2)}, u32[]{:S(2)}) collective-permute-start(bf16[8,32,512]{2,0,1:T(8,128)(2,1)} %bitcast.68), channel_id=1, source_target_pairs={{0,24},{4,28},{8,0},{12,4},{16,8},{20,12},{24,16},{28,20},{32,56},... | collective-permute-start | bytes 786440 | tf_op jit(solution)/shard_map/ppermute | solution.py:56
  19.8 12.2 %collective-permute-start.3 = (bf16[4,8,32,512]{3,1,2,0:T(8,128)(2,1)S(1)}, bf16[4,8,32,512]{3,1,2,0:T(8,128)(2,1)}, u32[]{:S(2)}, u32[]{:S(2)}) collective-permute-start(bf16[4,8,32,512]{3,1,2,0:T(8,128)(2,1)S(1)} %get-tuple-element.77), channel_id=1, source_target_pairs={{0,4},{4,0},{8,12},{12,8},{16,20},{20,16},{24,28},{28,24},{32,36},... | collective-permute-start | bytes 3145736 | tf_op jit(solution)/shard_map/ppermute | solution.py:56
  21.2 9.5 %collective-permute-start.12 = (f32[1,128]{1,0:T(1,128)S(1)}, f32[1,128]{1,0:T(1,128)S(1)}, u32[]{:S(2)}, u32[]{:S(2)}) collective-permute-start(f32[1,128]{1,0:T(1,128)S(1)} %dynamic-slice_bitcast_fusion.4), channel_id=1, source_target_pairs={{0,3},{1,0},{2,1},{3,2},{4,7},{5,4},{6,5},{7,6},{8,11},{9,8},{10,9... | collective-permute-start | bytes 1544 | tf_op jit(solution)/shard_map/ppermute | solution.py:64
  23.7 8.3 %collective-permute-start.11 = (f32[1,128]{1,0:T(1,128)S(1)}, f32[1,128]{1,0:T(1,128)S(1)}, u32[]{:S(2)}, u32[]{:S(2)}) collective-permute-start(f32[1,128]{1,0:T(1,128)S(1)} %dynamic-slice_bitcast_fusion.4), channel_id=1, source_target_pairs={{0,2},{1,3},{2,0},{3,1},{4,6},{5,7},{6,4},{7,5},{8,10},{9,11},{10,... | collective-permute-start | bytes 1544 | tf_op jit(solution)/shard_map/ppermute | solution.py:64
  24.2 7.8 %collective-permute-start.10 = (f32[1,128]{1,0:T(1,128)S(1)}, f32[1,128]{1,0:T(1,128)S(1)}, u32[]{:S(2)}, u32[]{:S(2)}) collective-permute-start(f32[1,128]{1,0:T(1,128)S(1)} %dynamic-slice_bitcast_fusion.4), channel_id=1, source_target_pairs={{0,1},{1,2},{2,3},{3,0},{4,5},{5,6},{6,7},{7,4},{8,9},{9,10},{10,1... | collective-permute-start | bytes 1544 | tf_op jit(solution)/shard_map/ppermute | solution.py:64
  27.2 16.1 %collective-permute-start.8 = (bf16[2048,128]{1,0:T(8,128)(2,1)}, bf16[2048,128]{1,0:T(8,128)(2,1)}, u32[]{:S(2)}, u32[]{:S(2)}) collective-permute-start(bf16[2048,128]{1,0:T(8,128)(2,1)} %dynamic_slice.44), channel_id=1, source_target_pairs={{0,3},{1,0},{2,1},{3,2},{4,7},{5,4},{6,5},{7,6},{8,11},{9,8},{10,9... | collective-permute-start | bytes 1572872 | tf_op jit(solution)/shard_map/ppermute | solution.py:64
  30.7 14.2 %collective-permute-start.7 = (bf16[2048,128]{1,0:T(8,128)(2,1)}, bf16[2048,128]{1,0:T(8,128)(2,1)}, u32[]{:S(2)}, u32[]{:S(2)}) collective-permute-start(bf16[2048,128]{1,0:T(8,128)(2,1)} %dynamic_slice.44), channel_id=1, source_target_pairs={{0,2},{1,3},{2,0},{3,1},{4,6},{5,7},{6,4},{7,5},{8,10},{9,11},{10,... | collective-permute-start | bytes 1572872 | tf_op jit(solution)/shard_map/ppermute | solution.py:64
  32.0 25.7 %collective-permute-start.6 = (bf16[2048,128]{1,0:T(8,128)(2,1)}, bf16[2048,128]{1,0:T(8,128)(2,1)}, u32[]{:S(2)}, u32[]{:S(2)}) collective-permute-start(bf16[2048,128]{1,0:T(8,128)(2,1)} %dynamic_slice.44), channel_id=1, source_target_pairs={{0,1},{1,2},{2,3},{3,0},{4,5},{5,6},{6,7},{7,4},{8,9},{9,10},{10,1... | collective-permute-start | bytes 1572872 | tf_op jit(solution)/shard_map/ppermute | solution.py:64
  38.7 21.9 %collective-permute-start.4 = (bf16[8,512]{1,0:T(8,128)(2,1)S(1)}, bf16[8,512]{1,0:T(8,128)(2,1)S(1)}, u32[]{:S(2)}, u32[]{:S(2)}) collective-permute-start(bf16[8,512]{1,0:T(8,128)(2,1)S(1)} %get-tuple-element.70), channel_id=1, source_target_pairs={{0,32},{4,36},{8,40},{12,44},{16,48},{20,52},{24,56},{28,60},{32,6... | collective-permute-start | bytes 24584 | tf_op jit(solution)/shard_map/ppermute | solution.py:56
  41.9 18.7 %collective-permute-start.5 = (bf16[8,512]{1,0:T(8,128)(2,1)S(1)}, bf16[8,512]{1,0:T(8,128)(2,1)S(1)}, u32[]{:S(2)}, u32[]{:S(2)}) collective-permute-start(bf16[8,512]{1,0:T(8,128)(2,1)S(1)} %get-tuple-element.71), channel_id=1, source_target_pairs={{32,0},{36,4},{40,8},{44,12},{48,16},{52,20},{56,24},{60,28},{64,3... | collective-permute-start | bytes 24584 | tf_op jit(solution)/shard_map/ppermute | solution.py:56
  59.2 29.8 %collective-permute-start.9 = (bf16[3,2048,128]{2,1,0:T(8,128)(2,1)S(1)}, bf16[3,2048,128]{2,1,0:T(8,128)(2,1)S(1)}, u32[]{:S(2)}, u32[]{:S(2)}) collective-permute-start(bf16[3,2048,128]{2,1,0:T(8,128)(2,1)S(1)} %pad_maximum_fusion.near_ref), channel_id=1, source_target_pairs={{0,4},{4,0},{8,12},{12,8},{16,20},{20,16},{24,28},{28,24},{32,36},... | collective-permute-start | bytes 4718600 | tf_op jit(solution)/shard_map/ppermute | solution.py:56
  87.0 2.0 %copy-start.2 = (bf16[2048,1024]{1,0:T(8,128)(2,1)}, bf16[2048,1024]{1,0:T(8,128)(2,1)S(1)}, u32[]{:S(2)}) copy-start(bf16[2048,1024]{1,0:T(8,128)(2,1)S(1)} %get-tuple-element.57.fl_ref) | copy-start | bytes 12582916
  119.0 9.4 %copy-start = (f32[2,512,512]{2,1,0:T(8,128)}, f32[2,512,512]{2,1,0:T(8,128)S(1)}, u32[]{:S(2)}) copy-start(f32[2,512,512]{2,1,0:T(8,128)S(1)} %products.2) | copy-start | bytes 6291460
  119.0 9.3 %collective-permute-start.13 = (f32[128,512]{1,0:T(8,128)S(1)}, f32[128,512]{1,0:T(8,128)S(1)}, u32[]{:S(2)}, u32[]{:S(2)}) collective-permute-start(f32[128,512]{1,0:T(8,128)S(1)} %get-tuple-element.66), channel_id=1, source_target_pairs={{0,32},{4,36},{8,40},{12,44},{16,48},{20,52},{24,56},{28,60},{32,6... | collective-permute-start | bytes 786440 | tf_op jit(solution)/shard_map/ppermute | solution.py:56
  120.4 8.0 %collective-permute-start.15 = (f32[128,512]{1,0:T(8,128)S(1)}, f32[128,512]{1,0:T(8,128)S(1)}, u32[]{:S(2)}, u32[]{:S(2)}) collective-permute-start(f32[128,512]{1,0:T(8,128)S(1)} %get-tuple-element.67), channel_id=1, source_target_pairs={{0,96},{4,100},{8,104},{12,108},{16,112},{20,116},{24,120},{28,124... | collective-permute-start | bytes 786440 | tf_op jit(solution)/shard_map/ppermute | solution.py:56
  121.9 12.0 %collective-permute-start.17 = (f32[128,512]{1,0:T(8,128)S(1)}, f32[128,512]{1,0:T(8,128)S(1)}, u32[]{:S(2)}, u32[]{:S(2)}) collective-permute-start(f32[128,512]{1,0:T(8,128)S(1)} %get-tuple-element.60), channel_id=1, source_target_pairs={{0,32},{4,36},{8,40},{12,44},{16,48},{20,52},{24,56},{28,60},{32,6... | collective-permute-start | bytes 786440 | tf_op jit(solution)/shard_map/ppermute | solution.py:56
  122.0 11.9 %collective-permute-start.19 = (f32[128,512]{1,0:T(8,128)S(1)}, f32[128,512]{1,0:T(8,128)S(1)}, u32[]{:S(2)}, u32[]{:S(2)}) collective-permute-start(f32[128,512]{1,0:T(8,128)S(1)} %get-tuple-element.61), channel_id=1, source_target_pairs={{0,96},{4,100},{8,104},{12,108},{16,112},{20,116},{24,120},{28,124... | collective-permute-start | bytes 786440 | tf_op jit(solution)/shard_map/ppermute | solution.py:56
  129.2 15.2 %collective-permute-start.14 = (f32[2,128,512]{2,1,0:T(8,128)}, f32[2,128,512]{2,1,0:T(8,128)S(1)}, u32[]{:S(2)}, u32[]{:S(2)}) collective-permute-start(f32[2,128,512]{2,1,0:T(8,128)} %get-tuple-element.64), channel_id=1, source_target_pairs={{0,32},{4,36},{8,40},{12,44},{16,48},{20,52},{24,56},{28,60},{32,6... | collective-permute-start | bytes 1572872 | tf_op jit(solution)/shard_map/ppermute | solution.py:56
  130.1 14.3 %collective-permute-start.16 = (f32[2,128,512]{2,1,0:T(8,128)}, f32[2,128,512]{2,1,0:T(8,128)S(1)}, u32[]{:S(2)}, u32[]{:S(2)}) collective-permute-start(f32[2,128,512]{2,1,0:T(8,128)} %get-tuple-element.65), channel_id=1, source_target_pairs={{0,96},{4,100},{8,104},{12,108},{16,112},{20,116},{24,120},{28,124... | collective-permute-start | bytes 1572872 | tf_op jit(solution)/shard_map/ppermute | solution.py:56
  134.9 20.9 %collective-permute-start.18 = (f32[2,128,512]{2,1,0:T(8,128)}, f32[2,128,512]{2,1,0:T(8,128)}, u32[]{:S(2)}, u32[]{:S(2)}) collective-permute-start(f32[2,128,512]{2,1,0:T(8,128)} %get-tuple-element.58), channel_id=1, source_target_pairs={{0,32},{4,36},{8,40},{12,44},{16,48},{20,52},{24,56},{28,60},{32,6... | collective-permute-start | bytes 1572872 | tf_op jit(solution)/shard_map/ppermute | solution.py:56
  135.8 20.0 %collective-permute-start.20 = (f32[2,128,512]{2,1,0:T(8,128)}, f32[2,128,512]{2,1,0:T(8,128)}, u32[]{:S(2)}, u32[]{:S(2)}) collective-permute-start(f32[2,128,512]{2,1,0:T(8,128)} %get-tuple-element.59), channel_id=1, source_target_pairs={{0,96},{4,100},{8,104},{12,108},{16,112},{20,116},{24,120},{28,124... | collective-permute-start | bytes 1572872 | tf_op jit(solution)/shard_map/ppermute | solution.py:56
  157.2 3.1 %collective-permute-start.21 = (f32[2,64,1024]{2,1,0:T(8,128)S(1)}, f32[2,64,1024]{2,1,0:T(8,128)S(1)}, u32[]{:S(2)}, u32[]{:S(2)}) collective-permute-start(f32[2,64,1024]{2,1,0:T(8,128)S(1)} %get-tuple-element.75), channel_id=1, source_target_pairs={{0,4},{4,0},{8,12},{12,8},{16,20},{20,16},{24,28},{28,24},{32,36},... | collective-permute-start | bytes 1572872 | tf_op jit(solution)/shard_map/ppermute | solution.py:56
